TPU v7x, 512 devices: a whole 4x4x16 slice. The times are simulated.
512 devices in a mesh: row: 32 (over z, core), col: 16 (over y, x).
Axes of the slice: x: 4, y: 4, z: 16, core: 2. Of those that a mesh axis runs over, the one named last changes fastest.
Arguments:
- a_blocks: bfloat16 [32, 16, 96, 128, 128], P('row', 'col'), may hold values from -0.5 to 0.5
- a_rows: int32 [32, 16, 96], P('row', 'col'), may hold values from 0 to 31, as said below
- a_cols: int32 [32, 16, 96], P('row', 'col'), may hold values from 0 to 63, as said below
- p_blocks: bfloat16 [1024, 128, 256], P(('row', 'col')), may hold values from -0.5 to 0.5
- coarse_slot: int32 [32, 16, 96, 4, 4], P('row', 'col'), may hold values from 0 to 127
Outputs:
- coarse_blocks: bfloat16 [32, 128, 4096], P('row', 'col')
Inputs may be any that keep to these rules, and one draw needn't show every extreme that they name: On each owner the pairs (a_rows, a_cols) of its 96 blocks are distinct. On each owner the pairs (a_rows, a_cols) of its 96 blocks are distinct.
All inputs are finite; a program needn't handle non-finite values.
Results may differ from a plain program's by a relative error of at most 0.0049.
Values may be sent and summed in bfloat16 or wider, within the bound.
A program may use at most 128 MiB of HBM per device.

v0:
```python
import jax
import jax.numpy as jnp
from jax import lax
from jax.sharding import PartitionSpec as P

KS_DEV = 8


def copy_for_each(array, axis):
    size = lax.axis_size(axis)
    return lax.all_to_all(
        jnp.broadcast_to(array[None], (size, *array.shape)), axis, 0, 0, tiled=True
    )


def joined_along(tiles, dim):
    lengths = list(tiles.shape[1:])
    lengths[dim] *= tiles.shape[0]
    return jnp.moveaxis(tiles, 0, dim).reshape(lengths)


def collect(array, axis, dim):
    tiles = copy_for_each(array, axis)
    return joined_along(tiles, dim)


def in_blocks(array, dim, size):
    lengths = array.shape
    tiles = array.reshape(*lengths[:dim], size, lengths[dim] // size, *lengths[dim + 1 :])
    return jnp.moveaxis(tiles, dim, 0)


def sum_at_owner(array, axis, dim):
    tiles = in_blocks(array, dim, lax.axis_size(axis))
    arrived = lax.all_to_all(tiles, axis, split_axis=0, concat_axis=0, tiled=True)
    return arrived.sum(axis=0)


def owner_terms(blocks, row_ids, col_ids, slot_ids, row_panel, column_panel, slot_count):
    count = blocks.shape[0]
    group_size = 16
    groups = count // group_size
    node_width = blocks.shape[1]
    panel_width = row_panel.shape[2]
    agg_blocks = slot_ids.shape[1]
    agg_width = panel_width // agg_blocks

    def accumulate(running, batch_item):
        blk, rws, cls, sls = batch_item
        right_rows = jnp.take(column_panel, cls, axis=0)
        product = jnp.einsum(
            "kab,kbw->kaw", blk, right_rows, preferred_element_type=jnp.float32
        ).astype(jnp.bfloat16)
        left_rows = jnp.take(row_panel, rws, axis=0)
        left_split = left_rows.reshape(group_size, node_width, agg_blocks, agg_width)
        right_split = product.reshape(group_size, node_width, agg_blocks, agg_width)
        contribs = jnp.einsum(
            "knta,knsb->ktsab", left_split, right_split, preferred_element_type=jnp.float32
        )
        contribs = contribs.reshape(group_size * agg_blocks * agg_blocks, agg_width * agg_width)
        running = running.at[sls.reshape(-1)].add(contribs)
        return (running, None)

    items = (
        blocks.reshape(groups, group_size, node_width, node_width),
        row_ids.reshape(groups, group_size),
        col_ids.reshape(groups, group_size),
        slot_ids.reshape(groups, group_size, agg_blocks, agg_blocks),
    )
    start = jnp.zeros((slot_count, agg_width * agg_width), jnp.float32)
    running, _ = lax.scan(accumulate, start, items)
    return running


def on_device(a_blocks, a_rows, a_cols, p_blocks, coarse_slot):
    rows_total = lax.axis_size("row")
    cols_total = lax.axis_size("col")
    fan_count = rows_total // cols_total
    piece_rows = p_blocks.shape[0]
    tail_shape = p_blocks.shape[1:]
    row_panel = collect(p_blocks, "col", 0)
    column_rows = lax.all_gather(p_blocks, "row", axis=0, tiled=True)
    grouped = column_rows.reshape((cols_total, fan_count, piece_rows) + tail_shape)
    regrouped = lax.all_to_all(grouped, "col", split_axis=0, concat_axis=2, tiled=True)
    column_panel = regrouped.reshape((fan_count * cols_total * piece_rows,) + tail_shape)
    slot_count = KS_DEV * cols_total
    running = owner_terms(
        a_blocks[0, 0],
        a_rows[0, 0],
        a_cols[0, 0],
        coarse_slot[0, 0],
        row_panel,
        column_panel,
        slot_count,
    )
    reduced = sum_at_owner(running, "col", 0)
    return reduced.astype(jnp.bfloat16)[None]


def solution(mesh):
    placed = (
        P("row", "col", None, None, None),
        P("row", "col", None),
        P("row", "col", None),
        P(("row", "col"), None, None),
        P("row", "col", None, None, None),
    )
    return jax.shard_map(
        on_device, mesh=mesh, in_specs=placed, out_specs=P("row", "col", None), check_vma=False
    )
```

profile of v0, /device:TPU:32, one launch (start us, length us, event | category | flops | bytes accessed | tf_op | source)
XLA Modules:
  0.0 480.8 jit_solution(17363315479896694393)
XLA Ops:
  7.3 80.4 %all-gather.2.cloned.1.call-done = bf16[64,128,256]{2,1,0:T(8,128)(2,1)} async-done(((bf16[2,128,256]{2,1,0:T(8,128)(2,1)}), bf16[64,128,256]{2,1,0:T(8,128)(2,1)}) %all-gather.2.cloned.1.call-update) | async-done | bytes 4194320 | tf_op jit(solution)/shard_map/all_gather | solution.py:82
  87.7 58.3 %all_to_all.25 = bf16[16,2,2,128,256]{4,3,2,1,0:T(8,128)(2,1)} all-to-all(bf16[16,2,2,128,256]{4,3,2,1,0:T(8,128)(2,1)} %bitcast.70), channel_id=1, replica_groups=mesh['row'=32,'col'=16] {'col'}, dimensions={0} | all-to-all | bytes 8388608 | tf_op jit(solution)/shard_map/all_to_all | solution.py:84
  147.5 3.7 all-to-all-start.1
  153.5 4.6 copy.25
  158.1 23.2 %all-to-all-done.1 = bf16[16,2,128,256]{3,2,1,0:T(8,128)(2,1)S(1)} async-done(((bf16[16,2,128,256]{3,2,1,0:T(8,128)(2,1)}), bf16[16,2,128,256]{3,2,1,0:T(8,128)(2,1)S(1)}, u32[]{:S(2)}, u32[]{:S(2)}) %all-to-all-start.1) | async-done | bytes 2097184 | tf_op jit(solution)/shard_map/all_to_all | solution.py:11
  182.8 257.3 %while.10 = (s32[]{:T(128)}, f32[128,4096]{1,0:T(8,128)S(1)}, s32[6,16,4,4]{3,2,1,0:T(4,128)S(1)}, bf16[6,16,128,128]{3,2,1,0:T(8,128)(2,1)}, s32[6,16]{1,0:T(8,...) while((s32[]{:T(128)}, f32[128,4096]{1,0:T(8,128)S(1)}, ...), condition=%wide.region_2.3_spmd, body=%wide.region_0.2_spmd.sunk | while | flops 405277728 | bytes 46678312 | solution.py:71
  182.9 2.8 gather_fusion
  194.0 6.1 %convolution_bitcast_fusion.2 = f32[16,4,4,64,64]{3,4,1,2,0:T(8,128)} fusion(bf16[16,128,4,64,1]{1,3,4,2,0:T(8,128)(2,1)} %bitcast.66, bf16[16,128,4,64]{1,3,2,0:T(8,128)(2,1)} %bitcast.67, pred[16]{0:T(512)(128)(4,1)S(1)} %get-tuple-element.156), kind=kOutput, calls=%fused_computation.3.clone.1 | convolution fusion | flops 268959744 | bytes 6291472 | tf_op jit(solution)/shard_map/while/body/eval_jaxpr/knta,knsb->ktsab/dot_general | solution.py:57
  200.1 9.3 %copy.35 = f32[16,4,4,64,64]{4,3,2,1,0:T(8,128)} copy(f32[16,4,4,64,64]{3,4,1,2,0:T(8,128)} %convolution_bitcast_fusion.2) | data formatting | bytes 8388608 | tf_op jit(solution)/shard_map/while/body/eval_jaxpr/knta,knsb->ktsab/transpose | solution.py:57
  209.4 7.9 %reshape.191 = f32[256,4096]{1,0:T(8,128)} reshape(f32[16,4,4,64,64]{4,3,2,1,0:T(8,128)} %copy.35) | data formatting | bytes 8388608 | tf_op jit(solution)/shard_map/while/body/eval_jaxpr/reshape | solution.py:60
  217.4 8.3 %scatter_fusion = f32[128,4096]{1,0:T(8,128)S(1)} fusion(f32[128,4096]{1,0:T(8,128)S(1)} %get-tuple-element.167, s32[256]{0:T(256)S(1)} %bitcast.73, f32[256,4096]{1,0:T(8,128)} %reshape.191), kind=kCustom, calls=%fused_computation.2.clone.1 | custom fusion | flops 1048576 | bytes 12583936 | tf_op jit(solution)/shard_map/while/body/eval_jaxpr/scatter-add | solution.py:61
  236.9 6.1 %convolution_bitcast_fusion.2 = f32[16,4,4,64,64]{3,4,1,2,0:T(8,128)} fusion(bf16[16,128,4,64,1]{1,3,4,2,0:T(8,128)(2,1)} %bitcast.66, bf16[16,128,4,64]{1,3,2,0:T(8,128)(2,1)} %bitcast.67, pred[16]{0:T(512)(128)(4,1)S(1)} %get-tuple-element.156), kind=kOutput, calls=%fused_computation.3.clone.1 | convolution fusion | flops 268959744 | bytes 6291472 | tf_op jit(solution)/shard_map/while/body/eval_jaxpr/knta,knsb->ktsab/dot_general | solution.py:57
  243.0 9.3 %copy.35 = f32[16,4,4,64,64]{4,3,2,1,0:T(8,128)} copy(f32[16,4,4,64,64]{3,4,1,2,0:T(8,128)} %convolution_bitcast_fusion.2) | data formatting | bytes 8388608 | tf_op jit(solution)/shard_map/while/body/eval_jaxpr/knta,knsb->ktsab/transpose | solution.py:57
  252.3 7.9 %reshape.191 = f32[256,4096]{1,0:T(8,128)} reshape(f32[16,4,4,64,64]{4,3,2,1,0:T(8,128)} %copy.35) | data formatting | bytes 8388608 | tf_op jit(solution)/shard_map/while/body/eval_jaxpr/reshape | solution.py:60
  260.3 8.3 %scatter_fusion = f32[128,4096]{1,0:T(8,128)S(1)} fusion(f32[128,4096]{1,0:T(8,128)S(1)} %get-tuple-element.167, s32[256]{0:T(256)S(1)} %bitcast.73, f32[256,4096]{1,0:T(8,128)} %reshape.191), kind=kCustom, calls=%fused_computation.2.clone.1 | custom fusion | flops 1048576 | bytes 12583936 | tf_op jit(solution)/shard_map/while/body/eval_jaxpr/scatter-add | solution.py:61
  279.8 6.1 %convolution_bitcast_fusion.2 = f32[16,4,4,64,64]{3,4,1,2,0:T(8,128)} fusion(bf16[16,128,4,64,1]{1,3,4,2,0:T(8,128)(2,1)} %bitcast.66, bf16[16,128,4,64]{1,3,2,0:T(8,128)(2,1)} %bitcast.67, pred[16]{0:T(512)(128)(4,1)S(1)} %get-tuple-element.156), kind=kOutput, calls=%fused_computation.3.clone.1 | convolution fusion | flops 268959744 | bytes 6291472 | tf_op jit(solution)/shard_map/while/body/eval_jaxpr/knta,knsb->ktsab/dot_general | solution.py:57
  285.9 9.3 %copy.35 = f32[16,4,4,64,64]{4,3,2,1,0:T(8,128)} copy(f32[16,4,4,64,64]{3,4,1,2,0:T(8,128)} %convolution_bitcast_fusion.2) | data formatting | bytes 8388608 | tf_op jit(solution)/shard_map/while/body/eval_jaxpr/knta,knsb->ktsab/transpose | solution.py:57
  295.2 7.9 %reshape.191 = f32[256,4096]{1,0:T(8,128)} reshape(f32[16,4,4,64,64]{4,3,2,1,0:T(8,128)} %copy.35) | data formatting | bytes 8388608 | tf_op jit(solution)/shard_map/while/body/eval_jaxpr/reshape | solution.py:60
  303.2 8.3 %scatter_fusion = f32[128,4096]{1,0:T(8,128)S(1)} fusion(f32[128,4096]{1,0:T(8,128)S(1)} %get-tuple-element.167, s32[256]{0:T(256)S(1)} %bitcast.73, f32[256,4096]{1,0:T(8,128)} %reshape.191), kind=kCustom, calls=%fused_computation.2.clone.1 | custom fusion | flops 1048576 | bytes 12583936 | tf_op jit(solution)/shard_map/while/body/eval_jaxpr/scatter-add | solution.py:61
  322.7 6.1 %convolution_bitcast_fusion.2 = f32[16,4,4,64,64]{3,4,1,2,0:T(8,128)} fusion(bf16[16,128,4,64,1]{1,3,4,2,0:T(8,128)(2,1)} %bitcast.66, bf16[16,128,4,64]{1,3,2,0:T(8,128)(2,1)} %bitcast.67, pred[16]{0:T(512)(128)(4,1)S(1)} %get-tuple-element.156), kind=kOutput, calls=%fused_computation.3.clone.1 | convolution fusion | flops 268959744 | bytes 6291472 | tf_op jit(solution)/shard_map/while/body/eval_jaxpr/knta,knsb->ktsab/dot_general | solution.py:57
  328.8 9.3 %copy.35 = f32[16,4,4,64,64]{4,3,2,1,0:T(8,128)} copy(f32[16,4,4,64,64]{3,4,1,2,0:T(8,128)} %convolution_bitcast_fusion.2) | data formatting | bytes 8388608 | tf_op jit(solution)/shard_map/while/body/eval_jaxpr/knta,knsb->ktsab/transpose | solution.py:57
  338.0 7.9 %reshape.191 = f32[256,4096]{1,0:T(8,128)} reshape(f32[16,4,4,64,64]{4,3,2,1,0:T(8,128)} %copy.35) | data formatting | bytes 8388608 | tf_op jit(solution)/shard_map/while/body/eval_jaxpr/reshape | solution.py:60
  346.1 8.3 %scatter_fusion = f32[128,4096]{1,0:T(8,128)S(1)} fusion(f32[128,4096]{1,0:T(8,128)S(1)} %get-tuple-element.167, s32[256]{0:T(256)S(1)} %bitcast.73, f32[256,4096]{1,0:T(8,128)} %reshape.191), kind=kCustom, calls=%fused_computation.2.clone.1 | custom fusion | flops 1048576 | bytes 12583936 | tf_op jit(solution)/shard_map/while/body/eval_jaxpr/scatter-add | solution.py:61
  365.6 6.1 %convolution_bitcast_fusion.2 = f32[16,4,4,64,64]{3,4,1,2,0:T(8,128)} fusion(bf16[16,128,4,64,1]{1,3,4,2,0:T(8,128)(2,1)} %bitcast.66, bf16[16,128,4,64]{1,3,2,0:T(8,128)(2,1)} %bitcast.67, pred[16]{0:T(512)(128)(4,1)S(1)} %get-tuple-element.156), kind=kOutput, calls=%fused_computation.3.clone.1 | convolution fusion | flops 268959744 | bytes 6291472 | tf_op jit(solution)/shard_map/while/body/eval_jaxpr/knta,knsb->ktsab/dot_general | solution.py:57
  371.7 9.3 %copy.35 = f32[16,4,4,64,64]{4,3,2,1,0:T(8,128)} copy(f32[16,4,4,64,64]{3,4,1,2,0:T(8,128)} %convolution_bitcast_fusion.2) | data formatting | bytes 8388608 | tf_op jit(solution)/shard_map/while/body/eval_jaxpr/knta,knsb->ktsab/transpose | solution.py:57
  380.9 7.9 %reshape.191 = f32[256,4096]{1,0:T(8,128)} reshape(f32[16,4,4,64,64]{4,3,2,1,0:T(8,128)} %copy.35) | data formatting | bytes 8388608 | tf_op jit(solution)/shard_map/while/body/eval_jaxpr/reshape | solution.py:60
  389.0 8.3 %scatter_fusion = f32[128,4096]{1,0:T(8,128)S(1)} fusion(f32[128,4096]{1,0:T(8,128)S(1)} %get-tuple-element.167, s32[256]{0:T(256)S(1)} %bitcast.73, f32[256,4096]{1,0:T(8,128)} %reshape.191), kind=kCustom, calls=%fused_computation.2.clone.1 | custom fusion | flops 1048576 | bytes 12583936 | tf_op jit(solution)/shard_map/while/body/eval_jaxpr/scatter-add | solution.py:61
  408.5 6.1 %convolution_bitcast_fusion.2 = f32[16,4,4,64,64]{3,4,1,2,0:T(8,128)} fusion(bf16[16,128,4,64,1]{1,3,4,2,0:T(8,128)(2,1)} %bitcast.66, bf16[16,128,4,64]{1,3,2,0:T(8,128)(2,1)} %bitcast.67, pred[16]{0:T(512)(128)(4,1)S(1)} %get-tuple-element.156), kind=kOutput, calls=%fused_computation.3.clone.1 | convolution fusion | flops 268959744 | bytes 6291472 | tf_op jit(solution)/shard_map/while/body/eval_jaxpr/knta,knsb->ktsab/dot_general | solution.py:57
  414.6 9.3 %copy.35 = f32[16,4,4,64,64]{4,3,2,1,0:T(8,128)} copy(f32[16,4,4,64,64]{3,4,1,2,0:T(8,128)} %convolution_bitcast_fusion.2) | data formatting | bytes 8388608 | tf_op jit(solution)/shard_map/while/body/eval_jaxpr/knta,knsb->ktsab/transpose | solution.py:57
  423.8 7.9 %reshape.191 = f32[256,4096]{1,0:T(8,128)} reshape(f32[16,4,4,64,64]{4,3,2,1,0:T(8,128)} %copy.35) | data formatting | bytes 8388608 | tf_op jit(solution)/shard_map/while/body/eval_jaxpr/reshape | solution.py:60
  431.8 8.3 %scatter_fusion = f32[128,4096]{1,0:T(8,128)S(1)} fusion(f32[128,4096]{1,0:T(8,128)S(1)} %get-tuple-element.167, s32[256]{0:T(256)S(1)} %bitcast.73, f32[256,4096]{1,0:T(8,128)} %reshape.191), kind=kCustom, calls=%fused_computation.2.clone.1 | custom fusion | flops 1048576 | bytes 12583936 | tf_op jit(solution)/shard_map/while/body/eval_jaxpr/scatter-add | solution.py:61
  440.1 31.4 %all_to_all.26 = f32[16,8,4096]{2,1,0:T(8,128)} all-to-all(f32[16,8,4096]{2,1,0:T(8,128)S(1)} %bitcast.65), channel_id=1, replica_groups=mesh['row'=32,'col'=16] {'col'}, dimensions={0} | all-to-all | bytes 4194304 | tf_op jit(solution)/shard_map/all_to_all | solution.py:35
  (92 shorter events, 73.3 us)
Async XLA Ops:
  6.5 81.2 %all-gather.2.cloned.1.call-start = ((), (), s32[]{:S(2)}) async-start(), calls=%async_computation.3 | async-start | bytes 4325376 | tf_op jit(solution)/shard_map/all_gather | solution.py:82
  87.7 58.3 %copy-start.1 = (bf16[2,128,256]{2,1,0:T(8,128)(2,1)S(1)}, bf16[2,128,256]{2,1,0:T(8,128)(2,1)}, u32[]{:S(2)}) copy-start(bf16[2,128,256]{2,1,0:T(8,128)(2,1)} %param.10) | copy-start | bytes 393220
  146.0 5.9 %copy-start.3 = (s32[1,1,96]{2,1,0:T(1,128)S(1)}, s32[1,1,96]{2,1,0:T(1,128)}, u32[]{:S(2)}) copy-start(s32[1,1,96]{2,1,0:T(1,128)} %param.9) | copy-start | bytes 1156
  146.0 6.6 %copy-start.4 = (s32[1,1,96]{2,1,0:T(1,128)S(1)}, s32[1,1,96]{2,1,0:T(1,128)}, u32[]{:S(2)}) copy-start(s32[1,1,96]{2,1,0:T(1,128)} %param.8) | copy-start | bytes 1156
  146.0 7.3 %copy-start.2 = (s32[1,1,96,4,4]{2,4,3,1,0:T(4,128)S(1)}, s32[1,1,96,4,4]{2,4,3,1,0:T(4,128)}, u32[]{:S(2)}) copy-start(s32[1,1,96,4,4]{2,4,3,1,0:T(4,128)} %param.11) | copy-start | bytes 18436
  147.5 33.7 %all-to-all-start.1 = ((bf16[16,2,128,256]{3,2,1,0:T(8,128)(2,1)}), bf16[16,2,128,256]{3,2,1,0:T(8,128)(2,1)S(1)}, u32[]{:S(2)}, u32[]{:S(2)}) async-start(bf16[16,2,128,256]{3,2,1,0:T(8,128)(2,1)} %broadcast_in_dim.32), calls=%async_computation.1 | async-start | bytes 4194304 | tf_op jit(solution)/shard_map/all_to_all | solution.py:11
  181.3 1.3 copy-start
Sparse Core Ops, SparseCore 0:
  9.5 78.1 all-gather.1
where the time goes:
time: 483 us; the launch traced here: 481 us
  local copies, waits for them, and re-layouts  164 us (34%)
  waiting for transfers between devices  104 us (22%)
  blocking collectives  89.7 us (19%)
  other arithmetic  53.6 us (11%)
  matrix products  51.7 us (11%)
  between operations  13.4 us (3%)
    all_gather x1, waiting for transfers between devices, on_device(): column_rows = lax.all_gather(p_blocks, 'row', axis=0, tiled=True)  80.4 us
    all_to_all x1, blocking collectives, on_device(): lax.all_to_all(grouped, 'col', split_axis=0, concat_axis=2, tiled=True)  58.3 us
    transpose x6, local copies, waits for them, and re-layouts, accumulate(): jnp.einsum('knta,knsb->ktsab', left_split, right_split, preferred_element...  55.5 us
    scatter-add x6, other arithmetic, accumulate(): running = running.at[sls.reshape(-1)].add(contribs)  49.7 us
    reshape x6, local copies, waits for them, and re-layouts, accumulate(): contribs.reshape(group_size * agg_blocks * agg_blocks, agg_width * agg_wi...  47.4 us
    dot_general x6, matrix products, accumulate(): jnp.einsum('knta,knsb->ktsab', left_split, right_split, preferred_element...  36.6 us
    all_to_all x1, blocking collectives, sum_at_owner(): lax.all_to_all(tiles, axis, split_axis=0, concat_axis=0, tiled=True)  31.4 us
    all_to_all x1, waiting for transfers between devices, copy_for_each(): lax.all_to_all(jnp.broadcast_to(array[None], (size, *array.shape)), axis,...  23.2 us
  transfers between devices with their start and end apart: 2, of which 2 were waited for; matrix products, arithmetic and copies ran while one was open for 1% of the time, Pallas kernels for 0%

commit v1 on v0

--- a/solution.py
+++ b/solution.py
@@ -79,7 +79,10 @@
     piece_rows = p_blocks.shape[0]
     tail_shape = p_blocks.shape[1:]
     row_panel = collect(p_blocks, "col", 0)
-    column_rows = lax.all_gather(p_blocks, "row", axis=0, tiled=True)
+    devices = lax.axis_size("row")
+    shards = jnp.stack([p_blocks for _ in range(devices)])
+    shards = lax.all_to_all(shards, "row", split_axis=0, concat_axis=0)
+    column_rows = jnp.concatenate(shards, axis=0)
     grouped = column_rows.reshape((cols_total, fan_count, piece_rows) + tail_shape)
     regrouped = lax.all_to_all(grouped, "col", split_axis=0, concat_axis=2, tiled=True)
     column_panel = regrouped.reshape((fan_count * cols_total * piece_rows,) + tail_shape)

time: 483 us -> 597 us (1.24)
  the two profiles are of different devices: /device:TPU:32 before, /device:TPU:64 now
where the time goes in v1:
time: 597 us; the launch traced here: 595 us
  blocking collectives  293 us (49%)
  local copies, waits for them, and re-layouts  165 us (28%)
  other arithmetic  53.5 us (9%)
  matrix products  51.8 us (9%)
  waiting for transfers between devices  26.1 us (4%)
    all_to_all x1, blocking collectives, on_device(): shards = lax.all_to_all(shards, 'row', split_axis=0, concat_axis=0)  201 us
    all_to_all x1, blocking collectives, on_device(): lax.all_to_all(grouped, 'col', split_axis=0, concat_axis=2, tiled=True)  60.6 us
    transpose x6, local copies, waits for them, and re-layouts, accumulate(): jnp.einsum('knta,knsb->ktsab', left_split, right_split, preferred_element...  55.6 us
    scatter-add x6, other arithmetic, accumulate(): running = running.at[sls.reshape(-1)].add(contribs)  49.7 us
    reshape x6, local copies, waits for them, and re-layouts, accumulate(): contribs.reshape(group_size * agg_blocks * agg_blocks, agg_width * agg_wi...  47.4 us
    dot_general x6, matrix products, accumulate(): jnp.einsum('knta,knsb->ktsab', left_split, right_split, preferred_element...  36.6 us
    all_to_all x1, blocking collectives, sum_at_owner(): lax.all_to_all(tiles, axis, split_axis=0, concat_axis=0, tiled=True)  31.3 us
    all_to_all x1, waiting for transfers between devices, copy_for_each(): lax.all_to_all(jnp.broadcast_to(array[None], (size, *array.shape)), axis,...  26.1 us
  transfers between devices with their start and end apart: 1, of which 1 were waited for; matrix products, arithmetic and copies ran while one was open for 1% of the time, Pallas kernels for 0%

profile of v1, /device:TPU:64, one launch (start us, length us, event | category | flops | bytes accessed | tf_op | source)
XLA Modules:
  0.0 594.6 jit_solution(9948372429511865811)
XLA Ops:
  1.4 201.2 %all_to_all.30 = bf16[32,2,128,256]{3,2,1,0:T(8,128)(2,1)S(1)} all-to-all(bf16[32,2,128,256]{3,2,1,0:T(8,128)(2,1)S(1)} %stack.2), channel_id=1, replica_groups=mesh['row'=32,'col'=16] {'row'}, dimensions={0} | all-to-all | bytes 8388608 | tf_op jit(solution)/shard_map/all_to_all | solution.py:84
  202.6 60.6 %all_to_all.31 = bf16[16,2,2,128,256]{4,3,2,1,0:T(8,128)(2,1)} all-to-all(bf16[16,2,2,128,256]{4,3,2,1,0:T(8,128)(2,1)S(1)} %bitcast.70), channel_id=1, replica_groups=mesh['row'=32,'col'=16] {'col'}, dimensions={0} | all-to-all | bytes 8388608 | tf_op jit(solution)/shard_map/all_to_all | solution.py:87
  264.8 4.1 all-to-all-start.2
  270.9 4.6 copy.14
  275.6 26.1 %all-to-all-done.2 = bf16[16,2,128,256]{3,2,1,0:T(8,128)(2,1)S(1)} async-done(((bf16[16,2,128,256]{3,2,1,0:T(8,128)(2,1)}), bf16[16,2,128,256]{3,2,1,0:T(8,128)(2,1)S(1)}, u32[]{:S(2)}, u32[]{:S(2)}) %all-to-all-start.2) | async-done | bytes 2097184 | tf_op jit(solution)/shard_map/all_to_all | solution.py:11
  303.2 257.7 %while.10 = (s32[]{:T(128)}, f32[128,4096]{1,0:T(8,128)S(1)}, s32[6,16,4,4]{3,2,1,0:T(4,128)S(1)}, bf16[6,16,128,128]{3,2,1,0:T(8,128)(2,1)}, s32[6,16]{1,0:T(8,...) while((s32[]{:T(128)}, f32[128,4096]{1,0:T(8,128)S(1)}, ...), condition=%wide.region_2.3_spmd, body=%wide.region_0.2_spmd.sunk | while | flops 405277728 | bytes 46678312 | solution.py:71
  303.2 2.8 gather_fusion
  314.5 6.1 %convolution_bitcast_fusion.2 = f32[16,4,4,64,64]{3,4,1,2,0:T(8,128)} fusion(bf16[16,128,4,64,1]{1,3,4,2,0:T(8,128)(2,1)} %bitcast.65, bf16[16,128,4,64]{1,3,2,0:T(8,128)(2,1)} %bitcast.66, pred[16]{0:T(512)(128)(4,1)S(1)} %get-tuple-element.140), kind=kOutput, calls=%fused_computation.3.clone.1 | convolution fusion | flops 268959744 | bytes 6291472 | tf_op jit(solution)/shard_map/while/body/eval_jaxpr/knta,knsb->ktsab/dot_general | solution.py:57
  320.6 9.3 %copy.24 = f32[16,4,4,64,64]{4,3,2,1,0:T(8,128)} copy(f32[16,4,4,64,64]{3,4,1,2,0:T(8,128)} %convolution_bitcast_fusion.2) | data formatting | bytes 8388608 | tf_op jit(solution)/shard_map/while/body/eval_jaxpr/knta,knsb->ktsab/transpose | solution.py:57
  329.8 7.9 %reshape.189 = f32[256,4096]{1,0:T(8,128)} reshape(f32[16,4,4,64,64]{4,3,2,1,0:T(8,128)} %copy.24) | data formatting | bytes 8388608 | tf_op jit(solution)/shard_map/while/body/eval_jaxpr/reshape | solution.py:60
  337.9 8.3 %scatter_fusion = f32[128,4096]{1,0:T(8,128)S(1)} fusion(f32[128,4096]{1,0:T(8,128)S(1)} %get-tuple-element.151, s32[256]{0:T(256)S(1)} %bitcast.73, f32[256,4096]{1,0:T(8,128)} %reshape.189), kind=kCustom, calls=%fused_computation.2.clone.1 | custom fusion | flops 1048576 | bytes 12583936 | tf_op jit(solution)/shard_map/while/body/eval_jaxpr/scatter-add | solution.py:61
  357.4 6.1 %convolution_bitcast_fusion.2 = f32[16,4,4,64,64]{3,4,1,2,0:T(8,128)} fusion(bf16[16,128,4,64,1]{1,3,4,2,0:T(8,128)(2,1)} %bitcast.65, bf16[16,128,4,64]{1,3,2,0:T(8,128)(2,1)} %bitcast.66, pred[16]{0:T(512)(128)(4,1)S(1)} %get-tuple-element.140), kind=kOutput, calls=%fused_computation.3.clone.1 | convolution fusion | flops 268959744 | bytes 6291472 | tf_op jit(solution)/shard_map/while/body/eval_jaxpr/knta,knsb->ktsab/dot_general | solution.py:57
  363.5 9.3 %copy.24 = f32[16,4,4,64,64]{4,3,2,1,0:T(8,128)} copy(f32[16,4,4,64,64]{3,4,1,2,0:T(8,128)} %convolution_bitcast_fusion.2) | data formatting | bytes 8388608 | tf_op jit(solution)/shard_map/while/body/eval_jaxpr/knta,knsb->ktsab/transpose | solution.py:57
  372.8 7.9 %reshape.189 = f32[256,4096]{1,0:T(8,128)} reshape(f32[16,4,4,64,64]{4,3,2,1,0:T(8,128)} %copy.24) | data formatting | bytes 8388608 | tf_op jit(solution)/shard_map/while/body/eval_jaxpr/reshape | solution.py:60
  380.8 8.3 %scatter_fusion = f32[128,4096]{1,0:T(8,128)S(1)} fusion(f32[128,4096]{1,0:T(8,128)S(1)} %get-tuple-element.151, s32[256]{0:T(256)S(1)} %bitcast.73, f32[256,4096]{1,0:T(8,128)} %reshape.189), kind=kCustom, calls=%fused_computation.2.clone.1 | custom fusion | flops 1048576 | bytes 12583936 | tf_op jit(solution)/shard_map/while/body/eval_jaxpr/scatter-add | solution.py:61
  400.4 6.1 %convolution_bitcast_fusion.2 = f32[16,4,4,64,64]{3,4,1,2,0:T(8,128)} fusion(bf16[16,128,4,64,1]{1,3,4,2,0:T(8,128)(2,1)} %bitcast.65, bf16[16,128,4,64]{1,3,2,0:T(8,128)(2,1)} %bitcast.66, pred[16]{0:T(512)(128)(4,1)S(1)} %get-tuple-element.140), kind=kOutput, calls=%fused_computation.3.clone.1 | convolution fusion | flops 268959744 | bytes 6291472 | tf_op jit(solution)/shard_map/while/body/eval_jaxpr/knta,knsb->ktsab/dot_general | solution.py:57
  406.5 9.3 %copy.24 = f32[16,4,4,64,64]{4,3,2,1,0:T(8,128)} copy(f32[16,4,4,64,64]{3,4,1,2,0:T(8,128)} %convolution_bitcast_fusion.2) | data formatting | bytes 8388608 | tf_op jit(solution)/shard_map/while/body/eval_jaxpr/knta,knsb->ktsab/transpose | solution.py:57
  415.7 7.9 %reshape.189 = f32[256,4096]{1,0:T(8,128)} reshape(f32[16,4,4,64,64]{4,3,2,1,0:T(8,128)} %copy.24) | data formatting | bytes 8388608 | tf_op jit(solution)/shard_map/while/body/eval_jaxpr/reshape | solution.py:60
  423.8 8.3 %scatter_fusion = f32[128,4096]{1,0:T(8,128)S(1)} fusion(f32[128,4096]{1,0:T(8,128)S(1)} %get-tuple-element.151, s32[256]{0:T(256)S(1)} %bitcast.73, f32[256,4096]{1,0:T(8,128)} %reshape.189), kind=kCustom, calls=%fused_computation.2.clone.1 | custom fusion | flops 1048576 | bytes 12583936 | tf_op jit(solution)/shard_map/while/body/eval_jaxpr/scatter-add | solution.py:61
  443.3 6.1 %convolution_bitcast_fusion.2 = f32[16,4,4,64,64]{3,4,1,2,0:T(8,128)} fusion(bf16[16,128,4,64,1]{1,3,4,2,0:T(8,128)(2,1)} %bitcast.65, bf16[16,128,4,64]{1,3,2,0:T(8,128)(2,1)} %bitcast.66, pred[16]{0:T(512)(128)(4,1)S(1)} %get-tuple-element.140), kind=kOutput, calls=%fused_computation.3.clone.1 | convolution fusion | flops 268959744 | bytes 6291472 | tf_op jit(solution)/shard_map/while/body/eval_jaxpr/knta,knsb->ktsab/dot_general | solution.py:57
  449.4 9.3 %copy.24 = f32[16,4,4,64,64]{4,3,2,1,0:T(8,128)} copy(f32[16,4,4,64,64]{3,4,1,2,0:T(8,128)} %convolution_bitcast_fusion.2) | data formatting | bytes 8388608 | tf_op jit(solution)/shard_map/while/body/eval_jaxpr/knta,knsb->ktsab/transpose | solution.py:57
  458.7 7.9 %reshape.189 = f32[256,4096]{1,0:T(8,128)} reshape(f32[16,4,4,64,64]{4,3,2,1,0:T(8,128)} %copy.24) | data formatting | bytes 8388608 | tf_op jit(solution)/shard_map/while/body/eval_jaxpr/reshape | solution.py:60
  466.7 8.3 %scatter_fusion = f32[128,4096]{1,0:T(8,128)S(1)} fusion(f32[128,4096]{1,0:T(8,128)S(1)} %get-tuple-element.151, s32[256]{0:T(256)S(1)} %bitcast.73, f32[256,4096]{1,0:T(8,128)} %reshape.189), kind=kCustom, calls=%fused_computation.2.clone.1 | custom fusion | flops 1048576 | bytes 12583936 | tf_op jit(solution)/shard_map/while/body/eval_jaxpr/scatter-add | solution.py:61
  486.3 6.1 %convolution_bitcast_fusion.2 = f32[16,4,4,64,64]{3,4,1,2,0:T(8,128)} fusion(bf16[16,128,4,64,1]{1,3,4,2,0:T(8,128)(2,1)} %bitcast.65, bf16[16,128,4,64]{1,3,2,0:T(8,128)(2,1)} %bitcast.66, pred[16]{0:T(512)(128)(4,1)S(1)} %get-tuple-element.140), kind=kOutput, calls=%fused_computation.3.clone.1 | convolution fusion | flops 268959744 | bytes 6291472 | tf_op jit(solution)/shard_map/while/body/eval_jaxpr/knta,knsb->ktsab/dot_general | solution.py:57
  492.4 9.3 %copy.24 = f32[16,4,4,64,64]{4,3,2,1,0:T(8,128)} copy(f32[16,4,4,64,64]{3,4,1,2,0:T(8,128)} %convolution_bitcast_fusion.2) | data formatting | bytes 8388608 | tf_op jit(solution)/shard_map/while/body/eval_jaxpr/knta,knsb->ktsab/transpose | solution.py:57
  501.6 7.9 %reshape.189 = f32[256,4096]{1,0:T(8,128)} reshape(f32[16,4,4,64,64]{4,3,2,1,0:T(8,128)} %copy.24) | data formatting | bytes 8388608 | tf_op jit(solution)/shard_map/while/body/eval_jaxpr/reshape | solution.py:60
  509.6 8.3 %scatter_fusion = f32[128,4096]{1,0:T(8,128)S(1)} fusion(f32[128,4096]{1,0:T(8,128)S(1)} %get-tuple-element.151, s32[256]{0:T(256)S(1)} %bitcast.73, f32[256,4096]{1,0:T(8,128)} %reshape.189), kind=kCustom, calls=%fused_computation.2.clone.1 | custom fusion | flops 1048576 | bytes 12583936 | tf_op jit(solution)/shard_map/while/body/eval_jaxpr/scatter-add | solution.py:61
  529.2 6.1 %convolution_bitcast_fusion.2 = f32[16,4,4,64,64]{3,4,1,2,0:T(8,128)} fusion(bf16[16,128,4,64,1]{1,3,4,2,0:T(8,128)(2,1)} %bitcast.65, bf16[16,128,4,64]{1,3,2,0:T(8,128)(2,1)} %bitcast.66, pred[16]{0:T(512)(128)(4,1)S(1)} %get-tuple-element.140), kind=kOutput, calls=%fused_computation.3.clone.1 | convolution fusion | flops 268959744 | bytes 6291472 | tf_op jit(solution)/shard_map/while/body/eval_jaxpr/knta,knsb->ktsab/dot_general | solution.py:57
  535.3 9.3 %copy.24 = f32[16,4,4,64,64]{4,3,2,1,0:T(8,128)} copy(f32[16,4,4,64,64]{3,4,1,2,0:T(8,128)} %convolution_bitcast_fusion.2) | data formatting | bytes 8388608 | tf_op jit(solution)/shard_map/while/body/eval_jaxpr/knta,knsb->ktsab/transpose | solution.py:57
  544.6 7.9 %reshape.189 = f32[256,4096]{1,0:T(8,128)} reshape(f32[16,4,4,64,64]{4,3,2,1,0:T(8,128)} %copy.24) | data formatting | bytes 8388608 | tf_op jit(solution)/shard_map/while/body/eval_jaxpr/reshape | solution.py:60
  552.6 8.3 %scatter_fusion = f32[128,4096]{1,0:T(8,128)S(1)} fusion(f32[128,4096]{1,0:T(8,128)S(1)} %get-tuple-element.151, s32[256]{0:T(256)S(1)} %bitcast.73, f32[256,4096]{1,0:T(8,128)} %reshape.189), kind=kCustom, calls=%fused_computation.2.clone.1 | custom fusion | flops 1048576 | bytes 12583936 | tf_op jit(solution)/shard_map/while/body/eval_jaxpr/scatter-add | solution.py:61
  560.9 31.3 %all_to_all.32 = f32[16,8,4096]{2,1,0:T(8,128)} all-to-all(f32[16,8,4096]{2,1,0:T(8,128)S(1)} %bitcast.64), channel_id=1, replica_groups=mesh['row'=32,'col'=16] {'col'}, dimensions={0} | all-to-all | bytes 4194304 | tf_op jit(solution)/shard_map/all_to_all | solution.py:35
  (91 shorter events, 74.0 us)
Async XLA Ops:
  202.6 60.6 %copy-start.1 = (bf16[2,128,256]{2,1,0:T(8,128)(2,1)S(1)}, bf16[2,128,256]{2,1,0:T(8,128)(2,1)}, u32[]{:S(2)}) copy-start(bf16[2,128,256]{2,1,0:T(8,128)(2,1)} %param.10) | copy-start | bytes 393220
  263.2 6.2 %copy-start.3 = (s32[1,1,96]{2,1,0:T(1,128)S(1)}, s32[1,1,96]{2,1,0:T(1,128)}, u32[]{:S(2)}) copy-start(s32[1,1,96]{2,1,0:T(1,128)} %param.9) | copy-start | bytes 1156
  263.2 6.9 %copy-start.4 = (s32[1,1,96]{2,1,0:T(1,128)S(1)}, s32[1,1,96]{2,1,0:T(1,128)}, u32[]{:S(2)}) copy-start(s32[1,1,96]{2,1,0:T(1,128)} %param.8) | copy-start | bytes 1156
  263.2 7.6 %copy-start.2 = (s32[1,1,96,4,4]{2,4,3,1,0:T(4,128)S(1)}, s32[1,1,96,4,4]{2,4,3,1,0:T(4,128)}, u32[]{:S(2)}) copy-start(s32[1,1,96,4,4]{2,4,3,1,0:T(4,128)} %param.11) | copy-start | bytes 18436
  264.8 36.9 %all-to-all-start.2 = ((bf16[16,2,128,256]{3,2,1,0:T(8,128)(2,1)}), bf16[16,2,128,256]{3,2,1,0:T(8,128)(2,1)S(1)}, u32[]{:S(2)}, u32[]{:S(2)}) async-start(bf16[16,2,128,256]{3,2,1,0:T(8,128)(2,1)} %broadcast_in_dim.32), calls=%async_computation.2 | async-start | bytes 4194304 | tf_op jit(solution)/shard_map/all_to_all | solution.py:11
  301.7 1.3 copy-start
